TPU v7x, 32 devices: a whole 2x2x4 slice. The times are simulated.
32 devices in a mesh: groups: 2 (over y), shard: 4 (over z), dp: 4 (over x, core).
Axes of the slice: x: 2, y: 2, z: 4, core: 2. Of those that a mesh axis runs over, the one named last changes fastest.
Arguments:
- maps_in: bfloat16 [32, 32, 1536], P(('groups', 'dp')), parts along dimension 0, may hold values from -6 to 6
- filters: bfloat16 [49, 1536], replicated, may hold values from -2 to 2
- w_expand: bfloat16 [1536, 6144], P(None, 'shard'), may hold values from -0.15625 to 0.15625
- w_project: bfloat16 [6144, 1536], P('shard'), may hold values from -0.078125 to 0.078125
- cotangent: bfloat16 [32, 32, 1536], P(('groups', 'dp')), parts along dimension 0, may hold values from -6 to 6
Outputs:
- block_out: bfloat16 [32, 32, 1536], P(('groups', 'dp')), parts along dimension 0
- grad_input: bfloat16 [32, 32, 1536], P(('groups', 'dp')), parts along dimension 0
- grad_expand: float32 [3072, 6144], P(('groups', 'dp'), 'shard'), parts along dimension 0
- grad_project: float32 [12288, 1536], P(('groups', 'shard'), 'dp'), parts along dimension 0
- grad_filters: float32 [98, 1536], P('groups'), parts along dimension 0
There are 2 independent parts, one for each index of `groups`. A program takes and returns all parts, laid end to end along the dimension named above; an argument that names none is the same for every part. Nothing has to cross between parts.
All inputs are finite; a program needn't handle non-finite values.
Results may differ from a plain program's by a relative error of at most 0.015.
Values may be sent and summed in bfloat16 or wider, within the bound.
A program may use at most 128 MiB of HBM per device.

v0:
```python
import jax
import jax.numpy as jnp
from jax import lax
from jax.sharding import PartitionSpec as P

KS = 7


def extended(block, sides, width):
    for axis, dim in sides:
        count = lax.axis_size(axis)
        forward = [(i, i + 1) for i in range(count - 1)]
        backward = [(target, source) for source, target in forward]
        low = lax.ppermute(
            lax.slice_in_dim(block, block.shape[dim] - width, None, axis=dim), axis, forward
        )
        high = lax.ppermute(lax.slice_in_dim(block, 0, width, axis=dim), axis, backward)
        block = jnp.concatenate([low, block, high], axis=dim)
    return block


def gelu_parts(hidden):
    cdf = 0.5 * (1.0 + jax.scipy.special.erf(hidden * 0.7071067811865476))
    density = jnp.exp(-0.5 * hidden * hidden) * 0.3989422804014327
    return (hidden * cdf, cdf + hidden * density)


def norm_stats(conv_rows):
    centered = conv_rows - jnp.mean(conv_rows, axis=-1, keepdims=True)
    variance = jnp.mean(centered * centered, axis=-1, keepdims=True)
    inv_scale = lax.rsqrt(variance + 1e-06)
    return (centered * inv_scale, inv_scale)


def norm_back(d_normed, scaled, inv_scale):
    first = jnp.mean(d_normed, axis=-1, keepdims=True)
    second = jnp.mean(d_normed * scaled, axis=-1, keepdims=True)
    return inv_scale * (d_normed - first - scaled * second)


def body(maps_in, filters, w_expand, w_project, cotangent):
    reach = KS // 2
    rows, cols, width = maps_in.shape
    count = rows * cols
    taps_f32 = filters.astype(jnp.float32)
    halo_in = extended(maps_in, (("dp", 0),), reach)
    padded_in = jnp.pad(halo_in, ((0, 0), (reach, reach), (0, 0)))
    conv_out = jnp.zeros((rows, cols, width), jnp.float32)
    for tap in range(KS * KS):
        tap_row, tap_col = divmod(tap, KS)
        conv_out = (
            conv_out
            + padded_in[tap_row : tap_row + rows, tap_col : tap_col + cols].astype(jnp.float32)
            * taps_f32[tap]
        )
    scaled, inv_scale = norm_stats(conv_out.reshape(count, width))
    normed = scaled.astype(jnp.bfloat16)
    hidden = jnp.dot(normed, w_expand, preferred_element_type=jnp.float32)
    activ, slope = gelu_parts(hidden)
    act = activ.astype(jnp.bfloat16)
    partial_out = jnp.dot(act, w_project, preferred_element_type=jnp.float32)
    cot_rows = cotangent.reshape(count, width)
    summed_out = lax.psum(partial_out.astype(jnp.bfloat16), "shard").astype(jnp.float32)
    d_act = lax.dot_general(
        cot_rows, w_project, (((1,), (1,)), ((), ())), preferred_element_type=jnp.float32
    )
    d_hidden = (d_act * slope).astype(jnp.bfloat16)
    grad_proj_local = lax.dot_general(
        act, cot_rows, (((0,), (0,)), ((), ())), preferred_element_type=jnp.float32
    )
    grad_exp_local = lax.dot_general(
        normed, d_hidden, (((0,), (0,)), ((), ())), preferred_element_type=jnp.float32
    )
    partial_norm = lax.dot_general(
        d_hidden, w_expand, (((1,), (1,)), ((), ())), preferred_element_type=jnp.float32
    )
    d_normed = lax.psum(partial_norm.astype(jnp.bfloat16), "shard").astype(jnp.float32)
    d_conv = norm_back(d_normed, scaled, inv_scale).astype(jnp.bfloat16)
    block_out = (
        (maps_in.reshape(count, width).astype(jnp.float32) + summed_out)
        .astype(jnp.bfloat16)
        .reshape(rows, cols, width)
    )
    grad_expand, grad_project = (
        lax.psum_scatter(
            grad_exp_local.astype(jnp.bfloat16), "dp", scatter_dimension=0, tiled=True
        ).astype(jnp.float32),
        lax.psum_scatter(
            grad_proj_local.astype(jnp.bfloat16), "dp", scatter_dimension=1, tiled=True
        ).astype(jnp.float32),
    )
    d_conv = d_conv.reshape(rows, cols, width)
    halo_grad = extended(d_conv, (("dp", 0),), reach)
    padded_grad = jnp.pad(halo_grad, ((0, 0), (reach, reach), (0, 0)))
    conv_grad = d_conv.astype(jnp.float32)
    back_sum = cotangent.astype(jnp.float32)
    filter_rows = []
    for tap in range(KS * KS):
        tap_row, tap_col = divmod(tap, KS)
        back_sum = (
            back_sum
            + padded_grad[
                2 * reach - tap_row : 2 * reach - tap_row + rows,
                2 * reach - tap_col : 2 * reach - tap_col + cols,
            ].astype(jnp.float32)
            * taps_f32[tap]
        )
        filter_rows.append(
            jnp.sum(
                conv_grad
                * padded_in[tap_row : tap_row + rows, tap_col : tap_col + cols].astype(jnp.float32),
                axis=(0, 1),
            )
        )
    grad_input = back_sum.astype(jnp.bfloat16)
    grad_filters = lax.psum(jnp.stack(filter_rows, axis=0).astype(jnp.bfloat16), "dp").astype(
        jnp.float32
    )
    return (block_out, grad_input, grad_expand, grad_project, grad_filters)


def solution(mesh):
    placed = (
        P(("groups", "dp"), None, None),
        P(),
        P(None, "shard"),
        P("shard", None),
        P(("groups", "dp"), None, None),
    )
    return jax.shard_map(
        body,
        mesh=mesh,
        in_specs=placed,
        out_specs=(
            P(("groups", "dp"), None, None),
            P(("groups", "dp"), None, None),
            P(("groups", "dp"), "shard"),
            P(("groups", "shard"), "dp"),
            P("groups", None),
        ),
        check_vma=False,
    )
```

profile of v0, /device:TPU:0, one launch (start us, length us, event | category | flops | bytes accessed | tf_op | source)
XLA Modules:
  0.0 244.9 jit_solution(9113310455872859118)
XLA Ops:
  8.4 2.4 collective-permute-start
  14.9 1.4 collective-permute-done.1
  16.9 9.2 %fusion.142 = (f32[4,32]{1,0:T(4,128)S(1)}, f32[4,32,1536]{2,1,0:T(8,128)S(1)}) fusion(f32[1536]{0:T(1024)S(1)} %get-tuple-element.66, bf16[10,38,1536]{2,1,0:T(8,128)(2,1)S(1)} %select_maximum_fusion.2, f32[1536]{0:T(1024)S(1)} %get-tuple-element.67, f32[1536]{0:T(1024)S(1)} %get-tuple-element.68, f32[1536]{0:T(1024)S(1)} %get-tuple-element.69, ...), kind=kLoop, calls=%fused_computation.326 | loop fusion | flops 28901248 | bytes 20355584 | tf_op jit(solution)/shard_map/reduce_sum | solution.py:29
  28.7 3.6 %fusion.146 = f32[128,1536]{1,0:T(8,128)S(1)} fusion(bf16[128,1536]{1,0:T(8,128)(2,1)S(1)} %fusion.136, bf16[1536,1536]{1,0:T(8,128)(2,1)} %param.7), kind=kOutput, calls=%fused_computation.329 | convolution fusion | flops 603979776 | bytes 5898240 | tf_op jit(solution)/shard_map/dot_general | solution.py:58
  32.3 4.2 %convolution_convert_fusion.3 = bf16[128,1536]{1,0:T(8,128)(2,1)} fusion(bf16[1536,1536]{1,0:T(8,128)(2,1)} %param.8, f32[128,1536]{1,0:T(8,128)S(1)} %fusion.146), kind=kOutput, calls=%fused_computation.57 | convolution fusion | flops 605159424 | bytes 5898240 | tf_op jit(solution)/shard_map/dot_general | solution.py:61
  36.6 1.7 fusion.1
  38.3 2.4 convolution_convert_fusion.2
  40.9 49.0 %all-reduce.8.cloned.1.call-done = (bf16[128,1536]{1,0:T(8,128)(2,1)}, bf16[128,1536]{1,0:T(8,128)(2,1)}) async-done(((bf16[128,1536]{1,0:T(8,128)(2,1)}, bf16[128,1536]{1,0:T(8,128)(2,1)}), (bf16[128,1536]{1,0:T(8,128)(2,1)}, bf16[128,1536]{1,0:T(8,128)(2,1)})) %all-reduce.8.cloned.1.call-update) | async-done | bytes 786448 | tf_op jit(solution)/shard_map/psum | solution.py:63
  89.9 1.3 convert_reduce_fusion
  91.2 3.5 %fusion.132 = (bf16[1536]{0:T(1024)(128)(2,1)S(1)}, bf16[1536]{0:T(1024)(128)(2,1)S(1)}, bf16[1536]{0:T(1024)(128)(2,1)S(1)}, bf16[1536]{0:T(1024)(128)(2,1)S(1)...) fusion(bf16[10,38,1536]{2,1,0:T(8,128)(2,1)S(1)} %select_maximu, ...), kind=kLoop, calls=%fused_computation.249 | loop fusion | flops 12358656 | bytes 8708096 | tf_op jit(solution)/shard_map/reduce_sum | solution.py:109
  96.0 2.0 fusion.111
  98.7 4.8 %stack.249 = bf16[49,1536]{1,0:T(8,128)(2,1)} concatenate(bf16[1,1536]{1,0:T(2,128)(2,1)S(1)} %stack.200, bf16[1,1536]{1,0:T(2,128)(2,1)S(1)} %stack.201, bf16[1,1536]{1,0:T(2,128)(2,1)S(1)} %stack.202, bf16[1,1536]{1,0:T(2,128)(2,1)S(1)} %stack.203, bf16[1,1536]{1,0:T(2,128)(2,1)S(1)} %stack.204, bf16[1,1536]{1,0:T(2,128)(2,1)S(1)} %stack.205, bf16[1,1536]{1,0:T(2,128)(2,1)S(1)} %stack.206, ...), dimensions={0} | concatenate | bytes 301056 | tf_op jit(solution)/shard_map/stack | solution.py:116
  103.6 3.6 %convolution_convert_fusion = bf16[1536,1536]{1,0:T(8,128)(2,1)} fusion(bf16[128,1536]{1,0:T(8,128)(2,1)S(1)} %bitcast.89, f32[128,1536]{1,0:T(8,128)S(1)} %copy-done.2), kind=kOutput, calls=%fused_computation.50 | convolution fusion | flops 607322112 | bytes 5898240 | tf_op jit(solution)/shard_map/dot_general | solution.py:68
  107.2 6.6 %copy.10 = bf16[1536,1536]{0,1:T(8,128)(2,1)} copy(bf16[1536,1536]{1,0:T(8,128)(2,1)} %convolution_convert_fusion) | data formatting | bytes 9437184
  115.0 3.6 %convolution_convert_fusion.1 = bf16[1536,1536]{1,0:T(8,128)(2,1)} fusion(bf16[128,1536]{1,0:T(8,128)(2,1)S(1)} %copy-done.6, bf16[128,1536]{1,0:T(8,128)(2,1)S(1)} %copy-done.10), kind=kOutput, calls=%fused_computation.51 | convolution fusion | flops 606339072 | bytes 5505024 | tf_op jit(solution)/shard_map/dot_general | solution.py:71
  119.0 1.9 collective-permute-start.2
  123.1 10.1 %all-reduce.6.cloned.1.call-done = bf16[49,1536]{1,0:T(8,128)(2,1)} async-done(((bf16[49,1536]{1,0:T(8,128)(2,1)}), bf16[49,1536]{1,0:T(8,128)(2,1)}) %all-reduce.6.cloned.1.call-update) | async-done | bytes 150544 | tf_op jit(solution)/shard_map/psum | solution.py:116
  133.2 1.7 convert_element_type.521
  135.6 7.4 %fusion.135 = bf16[4,32,1536]{2,1,0:T(8,128)(2,1)} fusion(bf16[4,32,1536]{2,1,0:T(8,128)(2,1)S(1)} %bitcast.85, bf16[4,32,1536]{2,1,0:T(8,128)(2,1)S(1)} %copy-done.8, bf16[3,32,1536]{2,1,0:T(8,128)(2,1)S(1)} %collective-permute-done.2, bf16[3,32,1536]{2,1,0:T(8,128)(2,1)S(1)} %collective-permute-done.3, bf16[10,38,1536]{2,1,0:T(8,128)(2,1)S(1)} %select_maximum_fusion, ...), kind=kLoop, calls=%fused_computation.257 | loop fusion | flops 30474240 | bytes 18585600 | tf_op jit(solution)/shard_map/convert_element_type | solution.py:115
  142.9 42.2 %reduce-scatter.7.cloned.1.call-done = bf16[384,1536]{1,0:T(8,128)(2,1)} async-done(((bf16[1536,1536]{1,0:T(8,128)(2,1)}), bf16[384,1536]{1,0:T(8,128)(2,1)}) %reduce-scatter.7.cloned.1.call-update) | async-done | bytes 1179664
  185.1 1.7 copy.11
  186.8 1.6 convert_element_type.520
  188.4 47.0 %reduce-scatter.5.cloned.1.call-done = bf16[384,1536]{1,0:T(8,128)(2,1)} async-done(((bf16[1536,1536]{1,0:T(8,128)(2,1)}), bf16[384,1536]{1,0:T(8,128)(2,1)}) %reduce-scatter.5.cloned.1.call-update) | async-done | bytes 1179664 | tf_op jit(solution)/shard_map/reduce_scatter | solution.py:85
  235.4 3.0 %convert_element_type.518 = f32[384,1536]{1,0:T(8,128)} convert(bf16[384,1536]{1,0:T(8,128)(2,1)} %reduce-scatter.5.cloned.1.call-done) | non-fusion elementwise | flops 589824 | bytes 3538944 | tf_op jit(solution)/shard_map/convert_element_type | solution.py:87
  (268 shorter events, 13.5 us)
Async XLA Ops:
  7.2 82.7 %all-reduce.8.cloned.1.call-start = ((), (), s32[]{:S(2)}) async-start(), calls=%async_computation.5 | async-start | bytes 1572864 | tf_op jit(solution)/shard_map/psum | solution.py:63
  8.4 6.4 %collective-permute-start = (bf16[3,32,1536]{2,1,0:T(8,128)(2,1)S(1)}, bf16[3,32,1536]{2,1,0:T(8,128)(2,1)S(1)}, u32[]{:S(2)}, u32[]{:S(2)}) collective-permute-start(bf16[3,32,1536]{2,1,0:T(8,128)(2,1)S(1)} %get-tuple-element.123), channel_id=1, source_target_pairs={{0,1},{1,2},{2,3},{4,5},{5,6},{6,7},{8,9},{9,10},{10,11},{12,13},{... | collective-permute-start | bytes 884744 | tf_op jit(solution)/shard_map/ppermute | solution.py:14
  10.7 5.6 %collective-permute-start.1 = (bf16[3,32,1536]{2,1,0:T(8,128)(2,1)S(1)}, bf16[3,32,1536]{2,1,0:T(8,128)(2,1)S(1)}, u32[]{:S(2)}, u32[]{:S(2)}) collective-permute-start(bf16[3,32,1536]{2,1,0:T(8,128)(2,1)S(1)} %get-tuple-element.124), channel_id=1, source_target_pairs={{1,0},{2,1},{3,2},{5,4},{6,5},{7,6},{9,8},{10,9},{11,10},{13,12},{... | collective-permute-start | bytes 884744 | tf_op jit(solution)/shard_map/ppermute | solution.py:17
  40.7 92.5 %all-reduce.6.cloned.1.call-start = ((), (), s32[]{:S(2)}) async-start(), calls=%async_computation.3 | async-start | bytes 344064 | tf_op jit(solution)/shard_map/psum | solution.py:116
  103.5 81.6 %reduce-scatter.7.cloned.1.call-start = ((), (), s32[]{:S(2)}) async-start(), calls=%async_computation.4 | async-start | bytes 5898240
  113.9 121.5 %reduce-scatter.5.cloned.1.call-start = ((), (), s32[]{:S(2)}) async-start(), calls=%async_computation.2 | async-start | bytes 5898240 | tf_op jit(solution)/shard_map/reduce_scatter | solution.py:85
  118.6 16.6 %copy-start.13 = (f32[1536]{0:T(1024)S(1)}, f32[1536]{0:T(1024)}, u32[]{:S(2)}) copy-start(f32[1536]{0:T(1024)} %copy-done.12) | copy-start | bytes 18436
  118.6 16.6 %copy-start.15 = (f32[1536]{0:T(1024)S(1)}, f32[1536]{0:T(1024)}, u32[]{:S(2)}) copy-start(f32[1536]{0:T(1024)} %copy-done.14) | copy-start | bytes 18436
  118.6 16.6 %copy-start.17 = (f32[1536]{0:T(1024)S(1)}, f32[1536]{0:T(1024)}, u32[]{:S(2)}) copy-start(f32[1536]{0:T(1024)} %copy-done.16) | copy-start | bytes 18436
  118.6 16.6 %copy-start.19 = (f32[1536]{0:T(1024)S(1)}, f32[1536]{0:T(1024)}, u32[]{:S(2)}) copy-start(f32[1536]{0:T(1024)} %copy-done.18) | copy-start | bytes 18436
  118.6 16.6 %copy-start.21 = (f32[1536]{0:T(1024)S(1)}, f32[1536]{0:T(1024)}, u32[]{:S(2)}) copy-start(f32[1536]{0:T(1024)} %copy-done.20) | copy-start | bytes 18436
  118.6 16.6 %copy-start.23 = (f32[1536]{0:T(1024)S(1)}, f32[1536]{0:T(1024)}, u32[]{:S(2)}) copy-start(f32[1536]{0:T(1024)} %copy-done.22) | copy-start | bytes 18436
  118.6 16.6 %copy-start.25 = (f32[1536]{0:T(1024)S(1)}, f32[1536]{0:T(1024)}, u32[]{:S(2)}) copy-start(f32[1536]{0:T(1024)} %copy-done.24) | copy-start | bytes 18436
  118.6 16.6 %copy-start.27 = (f32[1536]{0:T(1024)S(1)}, f32[1536]{0:T(1024)}, u32[]{:S(2)}) copy-start(f32[1536]{0:T(1024)} %copy-done.26) | copy-start | bytes 18436
  118.7 16.6 %copy-start.29 = (f32[1536]{0:T(1024)S(1)}, f32[1536]{0:T(1024)}, u32[]{:S(2)}) copy-start(f32[1536]{0:T(1024)} %copy-done.28) | copy-start | bytes 18436
  118.7 16.6 %copy-start.31 = (f32[1536]{0:T(1024)S(1)}, f32[1536]{0:T(1024)}, u32[]{:S(2)}) copy-start(f32[1536]{0:T(1024)} %copy-done.30) | copy-start | bytes 18436
  118.7 16.6 %copy-start.33 = (f32[1536]{0:T(1024)S(1)}, f32[1536]{0:T(1024)}, u32[]{:S(2)}) copy-start(f32[1536]{0:T(1024)} %copy-done.32) | copy-start | bytes 18436
  118.7 16.6 %copy-start.35 = (f32[1536]{0:T(1024)S(1)}, f32[1536]{0:T(1024)}, u32[]{:S(2)}) copy-start(f32[1536]{0:T(1024)} %copy-done.34) | copy-start | bytes 18436
  118.7 16.6 %copy-start.37 = (f32[1536]{0:T(1024)S(1)}, f32[1536]{0:T(1024)}, u32[]{:S(2)}) copy-start(f32[1536]{0:T(1024)} %copy-done.36) | copy-start | bytes 18436
  118.7 16.6 %copy-start.39 = (f32[1536]{0:T(1024)S(1)}, f32[1536]{0:T(1024)}, u32[]{:S(2)}) copy-start(f32[1536]{0:T(1024)} %copy-done.38) | copy-start | bytes 18436
  118.7 16.6 %copy-start.41 = (f32[1536]{0:T(1024)S(1)}, f32[1536]{0:T(1024)}, u32[]{:S(2)}) copy-start(f32[1536]{0:T(1024)} %copy-done.40) | copy-start | bytes 18436
  118.7 16.6 %copy-start.43 = (f32[1536]{0:T(1024)S(1)}, f32[1536]{0:T(1024)}, u32[]{:S(2)}) copy-start(f32[1536]{0:T(1024)} %copy-done.42) | copy-start | bytes 18436
  119.0 15.8 %collective-permute-start.2 = (bf16[3,32,1536]{2,1,0:T(8,128)(2,1)S(1)}, bf16[3,32,1536]{2,1,0:T(8,128)(2,1)S(1)}, u32[]{:S(2)}, u32[]{:S(2)}) collective-permute-start(bf16[3,32,1536]{2,1,0:T(8,128)(2,1)S(1)} %bitcast.93), channel_id=1, source_target_pairs={{0,1},{1,2},{2,3},{4,5},{5,6},{6,7},{8,9},{9,10},{10,11},{12,13},{... | collective-permute-start | bytes 884744 | tf_op jit(solution)/shard_map/ppermute | solution.py:14
  120.9 13.9 %collective-permute-start.3 = (bf16[3,32,1536]{2,1,0:T(8,128)(2,1)S(1)}, bf16[3,32,1536]{2,1,0:T(8,128)(2,1)S(1)}, u32[]{:S(2)}, u32[]{:S(2)}) collective-permute-start(bf16[3,32,1536]{2,1,0:T(8,128)(2,1)S(1)} %bitcast.92), channel_id=1, source_target_pairs={{1,0},{2,1},{3,2},{5,4},{6,5},{7,6},{9,8},{10,9},{11,10},{13,12},{... | collective-permute-start | bytes 884744 | tf_op jit(solution)/shard_map/ppermute | solution.py:17
  (76 other events, 711.7 us)
Sparse Core Ops, SparseCore 0:
  40.8 49.0 all-reduce.7
  103.6 29.4 all-reduce.5
  135.9 49.2 reduce-scatter.6
  187.5 47.8 reduce-scatter.4
where the time goes:
time: 245 us
  waiting for transfers between devices  150 us (61%)
  other arithmetic  34.5 us (14%)
  matrix products  19 us (8%)
  local copies, waits for them, and re-layouts  18.7 us (8%)
  between operations  15.7 us (6%)
  starting transfers between devices  7.21 us (3%)
    psum x1, waiting for transfers between devices, body(): lax.psum(partial_out.astype(jnp.bfloat16), 'shard').astype(jnp.float32)  49 us
    reduce_scatter x1, waiting for transfers between devices, body(): lax.psum_scatter(grad_exp_local.astype(jnp.bfloat16), 'dp', scatter_dimen...  47 us
    unnamed x5, waiting for transfers between devices  42.3 us
    psum x1, waiting for transfers between devices, body(): lax.psum(jnp.stack(filter_rows, axis=0).astype(jnp.bfloat16), 'dp')  10.1 us
    unnamed x187, local copies, waits for them, and re-layouts  9.8 us
    reduce_sum x1, other arithmetic, norm_stats(): centered = conv_rows - jnp.mean(conv_rows, axis=-1, keepdims=True)  9.17 us
    convert_element_type x1, other arithmetic, body(): grad_input = back_sum.astype(jnp.bfloat16)  7.36 us
    reduce_sum x3, other arithmetic, body(): jnp.sum(conv_grad * padded_in[tap_row:tap_row + rows, tap_col:tap_col + c...  6.76 us
  transfers between devices with their start and end apart: 8, of which 5 were waited for; matrix products, arithmetic and copies ran while one was open for 12% of the time, Pallas kernels for 0%

commit v1 on v0

--- a/solution.py
+++ b/solution.py
@@ -4,6 +4,11 @@
 from jax.sharding import PartitionSpec as P
 
 KS = 7
+
+
+def numbers_meet(shard_in):
+    later = jax.lax.all_gather(shard_in, axis_name="dp")
+    return jnp.sum(later, axis=0)
 
 
 def extended(block, sides, width):
@@ -113,7 +118,7 @@
             )
         )
     grad_input = back_sum.astype(jnp.bfloat16)
-    grad_filters = lax.psum(jnp.stack(filter_rows, axis=0).astype(jnp.bfloat16), "dp").astype(
+    grad_filters = numbers_meet(jnp.stack(filter_rows, axis=0).astype(jnp.bfloat16)).astype(
         jnp.float32
     )
     return (block_out, grad_input, grad_expand, grad_project, grad_filters)

time: 245 us -> 171 us (0.70)
  waiting for transfers between devices: 150 us -> 67.2 us
  blocking collectives: 0 us -> 9.04 us
  local copies, waits for them, and re-layouts: 18.7 us -> 14.2 us
    unnamed x5 -> x4, waiting for transfers between devices: 42.3 us -> 0.05 us
    psum x1, waiting for transfers between devices: 49 us -> 32.8 us  [body(): lax.psum(partial_out.astype(jnp.bfloat16), 'shard').astype(jnp.float32)]
    reduce_scatter x1, waiting for transfers between devices: 47 us -> 31.5 us  [body(): lax.psum_scatter(grad_exp_local.astype(jnp.bfloat16), 'dp', scatter_dimen...]
    psum x1 -> x0, waiting for transfers between devices: 10.1 us -> none  [body(): lax.psum(jnp.stack(filter_rows, axis=0).astype(jnp.bfloat16), 'dp')]
    all_gather x0 -> x1, blocking collectives: none -> 9.04 us  [numbers_meet(): later = jax.lax.all_gather(shard_in, axis_name='dp')]
    another operation x50, local copies, waits for them, and re-layouts: 5.07 us -> 0.86 us  [body(): jnp.stack(filter_rows, axis=0).astype(jnp.bfloat16)]
    unnamed x187 -> x183, local copies, waits for them, and re-layouts: 9.8 us -> 9.49 us
  transfers between devices with their start and end apart: 8 -> 7, of which waited for: 5 -> 4; matrix products, arithmetic and copies ran while one was open for 12% -> 24% of each run, Pallas kernels for 0% -> 0%
where the time goes in v1:
time: 171 us; the launch traced here: 170 us
  waiting for transfers between devices  67.2 us (39%)
  other arithmetic  33.7 us (20%)
  matrix products  21.1 us (12%)
  between operations  17.3 us (10%)
  local copies, waits for them, and re-layouts  14.2 us (8%)
  blocking collectives  9.04 us (5%)
  starting transfers between devices  7.54 us (4%)
    psum x1, waiting for transfers between devices, body(): lax.psum(partial_out.astype(jnp.bfloat16), 'shard').astype(jnp.float32)  32.8 us
    reduce_scatter x1, waiting for transfers between devices, body(): lax.psum_scatter(grad_exp_local.astype(jnp.bfloat16), 'dp', scatter_dimen...  31.5 us
    unnamed x183, local copies, waits for them, and re-layouts  9.49 us
    reduce_sum x1, other arithmetic, norm_stats(): centered = conv_rows - jnp.mean(conv_rows, axis=-1, keepdims=True)  9.17 us
    all_gather x1, blocking collectives, numbers_meet(): later = jax.lax.all_gather(shard_in, axis_name='dp')  9.04 us
    convert_element_type x1, other arithmetic, body(): grad_input = back_sum.astype(jnp.bfloat16)  7.37 us
    reduce_sum x3, other arithmetic, body(): jnp.sum(conv_grad * padded_in[tap_row:tap_row + rows, tap_col:tap_col + c...  6.76 us
    dot_general x1, matrix products, body(): lax.dot_general(act, cot_rows, (((0,), (0,)), ((), ())), preferred_elemen...  4.84 us
  transfers between devices with their start and end apart: 7, of which 4 were waited for; matrix products, arithmetic and copies ran while one was open for 24% of the time, Pallas kernels for 0%

profile of v1, /device:TPU:0, one launch (start us, length us, event | category | flops | bytes accessed | tf_op | source)
XLA Modules:
  0.0 170.1 jit_solution(13511883203734515055)
XLA Ops:
  9.2 2.4 %collective-permute-start = (bf16[3,32,1536]{2,1,0:T(8,128)(2,1)S(1)}, bf16[3,32,1536]{2,1,0:T(8,128)(2,1)S(1)}, u32[]{:S(2)}, u32[]{:S(2)}) collective-permute-start(bf16[3,32,1536]{2,1,0:T(8,128)(2,1)S(1)} %get-tuple-element.123), channel_id=1, source_target_pairs={{0,1},{1,2},{2,3},{4,5},{5,6},{6,7},{8,9},{9,10},{10,11},{12,13},{... | collective-permute-start | bytes 884744 | tf_op jit(solution)/shard_map/ppermute | solution.py:19
  11.6 1.3 collective-permute-start.1
  15.7 1.4 collective-permute-done.1
  17.7 9.2 %fusion.142 = (f32[4,32]{1,0:T(4,128)S(1)}, f32[4,32,1536]{2,1,0:T(8,128)S(1)}) fusion(f32[1536]{0:T(1024)S(1)} %get-tuple-element.66, bf16[10,38,1536]{2,1,0:T(8,128)(2,1)S(1)} %select_maximum_fusion.2, f32[1536]{0:T(1024)S(1)} %get-tuple-element.67, f32[1536]{0:T(1024)S(1)} %get-tuple-element.68, f32[1536]{0:T(1024)S(1)} %get-tuple-element.69, ...), kind=kLoop, calls=%fused_computation.326 | loop fusion | flops 28901248 | bytes 20355584 | tf_op jit(solution)/shard_map/reduce_sum | solution.py:34
  29.5 3.5 %fusion.146 = f32[128,1536]{1,0:T(8,128)S(1)} fusion(bf16[128,1536]{1,0:T(8,128)(2,1)S(1)} %fusion.136, bf16[1536,1536]{1,0:T(8,128)(2,1)} %param.7), kind=kOutput, calls=%fused_computation.329 | convolution fusion | flops 603979776 | bytes 5898240 | tf_op jit(solution)/shard_map/dot_general | solution.py:63
  33.0 4.2 %convolution_convert_fusion.3 = bf16[128,1536]{1,0:T(8,128)(2,1)} fusion(bf16[1536,1536]{1,0:T(8,128)(2,1)} %param.8, f32[128,1536]{1,0:T(8,128)S(1)} %fusion.146), kind=kOutput, calls=%fused_computation.57 | convolution fusion | flops 605159424 | bytes 5898240 | tf_op jit(solution)/shard_map/dot_general | solution.py:66
  37.3 1.6 fusion.1
  39.7 2.4 %convolution_convert_fusion.2 = bf16[128,1536]{1,0:T(8,128)(2,1)} fusion(bf16[128,1536]{1,0:T(8,128)(2,1)S(1)} %fusion.1, bf16[1536,1536]{1,0:T(8,128)(2,1)S(1)} %bitcast.82), kind=kOutput, calls=%fused_computation.56 | convolution fusion | flops 604176384 | bytes 5505024 | tf_op jit(solution)/shard_map/dot_general | solution.py:79
  42.2 4.8 %convolution_convert_fusion = bf16[1536,1536]{1,0:T(8,128)(2,1)} fusion(bf16[128,1536]{1,0:T(8,128)(2,1)} %bitcast.88, f32[128,1536]{1,0:T(8,128)} %copy-done.1), kind=kOutput, calls=%fused_computation.50 | convolution fusion | flops 607322112 | bytes 5898240 | tf_op jit(solution)/shard_map/dot_general | solution.py:73
  47.0 6.6 %copy.10 = bf16[1536,1536]{0,1:T(8,128)(2,1)} copy(bf16[1536,1536]{1,0:T(8,128)(2,1)} %convolution_convert_fusion) | data formatting | bytes 9437184
  53.9 4.6 %convolution_convert_fusion.1 = bf16[1536,1536]{1,0:T(8,128)(2,1)} fusion(bf16[128,1536]{1,0:T(8,128)(2,1)S(1)} %fusion.136, bf16[128,1536]{1,0:T(8,128)(2,1)} %copy-done.6), kind=kOutput, calls=%fused_computation.51 | convolution fusion | flops 606339072 | bytes 5505024 | tf_op jit(solution)/shard_map/dot_general | solution.py:76
  58.5 32.8 %all-reduce.5.cloned.1.call-done = (bf16[128,1536]{1,0:T(8,128)(2,1)}, bf16[128,1536]{1,0:T(8,128)(2,1)}) async-done(((bf16[128,1536]{1,0:T(8,128)(2,1)}, bf16[128,1536]{1,0:T(8,128)(2,1)}), (bf16[128,1536]{1,0:T(8,128)(2,1)}, bf16[128,1536]{1,0:T(8,128)(2,1)})) %all-reduce.5.cloned.1.call-update) | async-done | bytes 786448 | tf_op jit(solution)/shard_map/psum | solution.py:68
  91.3 1.3 convert_reduce_fusion
  92.6 3.5 %fusion.132 = (bf16[1536]{0:T(1024)(128)(2,1)S(1)}, bf16[1536]{0:T(1024)(128)(2,1)S(1)}, bf16[1536]{0:T(1024)(128)(2,1)S(1)}, bf16[1536]{0:T(1024)(128)(2,1)S(1)...) fusion(bf16[10,38,1536]{2,1,0:T(8,128)(2,1)S(1)} %select_maximu, ...), kind=kLoop, calls=%fused_computation.249 | loop fusion | flops 12358656 | bytes 8708096 | tf_op jit(solution)/shard_map/reduce_sum | solution.py:114
  97.4 2.0 %fusion.111 = (bf16[1536]{0:T(1024)(128)(2,1)S(1)}, bf16[1536]{0:T(1024)(128)(2,1)S(1)}, bf16[1536]{0:T(1024)(128)(2,1)S(1)}, bf16[1536]{0:T(1024)(128)(2,1)S(1)...) fusion(bf16[10,38,1536]{2,1,0:T(8,128)(2,1)S(1)} %select_maximu, ...), kind=kLoop, calls=%fused_computation.228 | loop fusion | flops 10785792 | bytes 7526400 | tf_op jit(solution)/shard_map/reduce_sum | solution.py:114
  100.7 9.0 %all_gather.4 = bf16[4,49,1536]{2,1,0:T(8,128)(2,1)S(1)} all-gather(bf16[1,49,1536]{2,1,0:T(8,128)(2,1)S(1)} %stack.199), channel_id=1, replica_groups=mesh['groups'=2,'shard'=4,'dp'=4] {'dp'}, dimensions={0}, use_global_device_ids=true | all-gather | bytes 752640 | tf_op jit(solution)/shard_map/all_gather | solution.py:10
  111.0 2.3 %collective-permute-start.2 = (bf16[3,32,1536]{2,1,0:T(8,128)(2,1)S(1)}, bf16[3,32,1536]{2,1,0:T(8,128)(2,1)S(1)}, u32[]{:S(2)}, u32[]{:S(2)}) collective-permute-start(bf16[3,32,1536]{2,1,0:T(8,128)(2,1)S(1)} %bitcast.93), channel_id=1, source_target_pairs={{0,1},{1,2},{2,3},{4,5},{5,6},{6,7},{8,9},{9,10},{10,11},{12,13},{... | collective-permute-start | bytes 884744 | tf_op jit(solution)/shard_map/ppermute | solution.py:19
  113.3 1.3 collective-permute-start.3
  115.5 1.3 collective-permute-done.3
  117.6 7.4 %fusion.135 = bf16[4,32,1536]{2,1,0:T(8,128)(2,1)} fusion(bf16[4,32,1536]{2,1,0:T(8,128)(2,1)S(1)} %bitcast.85, bf16[4,32,1536]{2,1,0:T(8,128)(2,1)S(1)} %copy-done.5, bf16[3,32,1536]{2,1,0:T(8,128)(2,1)S(1)} %collective-permute-done.2, bf16[3,32,1536]{2,1,0:T(8,128)(2,1)S(1)} %collective-permute-done.3, bf16[10,38,1536]{2,1,0:T(8,128)(2,1)S(1)} %select_maximum_fusion, ...), kind=kLoop, calls=%fused_computation.257 | loop fusion | flops 30474240 | bytes 18585600 | tf_op jit(solution)/shard_map/convert_element_type | solution.py:120
  124.9 1.7 copy.11
  126.6 1.6 convert_element_type.529
  128.2 31.5 %reduce-scatter.5.cloned.1.call-done = bf16[384,1536]{1,0:T(8,128)(2,1)} async-done(((bf16[1536,1536]{1,0:T(8,128)(2,1)}), bf16[384,1536]{1,0:T(8,128)(2,1)}) %reduce-scatter.5.cloned.1.call-update) | async-done | bytes 1179664 | tf_op jit(solution)/shard_map/reduce_scatter | solution.py:90
  159.7 3.0 %convert_element_type.527 = f32[384,1536]{1,0:T(8,128)} convert(bf16[384,1536]{1,0:T(8,128)(2,1)} %reduce-scatter.5.cloned.1.call-done) | non-fusion elementwise | flops 589824 | bytes 3538944 | tf_op jit(solution)/shard_map/convert_element_type | solution.py:92
  (263 shorter events, 12.1 us)
Async XLA Ops:
  8.0 83.3 %all-reduce.5.cloned.1.call-start = ((), (), s32[]{:S(2)}) async-start(), calls=%async_computation.4 | async-start | bytes 1572864 | tf_op jit(solution)/shard_map/psum | solution.py:68
  9.2 6.4 %collective-permute-start = (bf16[3,32,1536]{2,1,0:T(8,128)(2,1)S(1)}, bf16[3,32,1536]{2,1,0:T(8,128)(2,1)S(1)}, u32[]{:S(2)}, u32[]{:S(2)}) collective-permute-start(bf16[3,32,1536]{2,1,0:T(8,128)(2,1)S(1)} %get-tuple-element.123), channel_id=1, source_target_pairs={{0,1},{1,2},{2,3},{4,5},{5,6},{6,7},{8,9},{9,10},{10,11},{12,13},{... | collective-permute-start | bytes 884744 | tf_op jit(solution)/shard_map/ppermute | solution.py:19
  11.6 5.6 %collective-permute-start.1 = (bf16[3,32,1536]{2,1,0:T(8,128)(2,1)S(1)}, bf16[3,32,1536]{2,1,0:T(8,128)(2,1)S(1)}, u32[]{:S(2)}, u32[]{:S(2)}) collective-permute-start(bf16[3,32,1536]{2,1,0:T(8,128)(2,1)S(1)} %get-tuple-element.124), channel_id=1, source_target_pairs={{1,0},{2,1},{3,2},{5,4},{6,5},{7,6},{9,8},{10,9},{11,10},{13,12},{... | collective-permute-start | bytes 884744 | tf_op jit(solution)/shard_map/ppermute | solution.py:22
  15.5 11.5 %copy-start.56 = (f32[1536]{0:T(1024)}, f32[1536]{0:T(1024)S(1)}, u32[]{:S(2)}) copy-start(f32[1536]{0:T(1024)S(1)} %get-tuple-element.86) | copy-start | bytes 18436
  15.5 11.5 %copy-start.58 = (f32[1536]{0:T(1024)}, f32[1536]{0:T(1024)S(1)}, u32[]{:S(2)}) copy-start(f32[1536]{0:T(1024)S(1)} %get-tuple-element.87) | copy-start | bytes 18436
  15.5 11.5 %copy-start.60 = (f32[1536]{0:T(1024)}, f32[1536]{0:T(1024)S(1)}, u32[]{:S(2)}) copy-start(f32[1536]{0:T(1024)S(1)} %get-tuple-element.88) | copy-start | bytes 18436
  15.5 11.5 %copy-start.62 = (f32[1536]{0:T(1024)}, f32[1536]{0:T(1024)S(1)}, u32[]{:S(2)}) copy-start(f32[1536]{0:T(1024)S(1)} %get-tuple-element.89) | copy-start | bytes 18436
  15.5 11.5 %copy-start.64 = (f32[1536]{0:T(1024)}, f32[1536]{0:T(1024)S(1)}, u32[]{:S(2)}) copy-start(f32[1536]{0:T(1024)S(1)} %get-tuple-element.90) | copy-start | bytes 18436
  15.5 11.5 %copy-start.66 = (f32[1536]{0:T(1024)}, f32[1536]{0:T(1024)S(1)}, u32[]{:S(2)}) copy-start(f32[1536]{0:T(1024)S(1)} %get-tuple-element.91) | copy-start | bytes 18436
  15.5 11.5 %copy-start.68 = (f32[1536]{0:T(1024)}, f32[1536]{0:T(1024)S(1)}, u32[]{:S(2)}) copy-start(f32[1536]{0:T(1024)S(1)} %get-tuple-element.92) | copy-start | bytes 18436
  15.5 11.5 %copy-start.70 = (f32[1536]{0:T(1024)}, f32[1536]{0:T(1024)S(1)}, u32[]{:S(2)}) copy-start(f32[1536]{0:T(1024)S(1)} %get-tuple-element.93) | copy-start | bytes 18436
  15.5 11.5 %copy-start.72 = (f32[1536]{0:T(1024)}, f32[1536]{0:T(1024)S(1)}, u32[]{:S(2)}) copy-start(f32[1536]{0:T(1024)S(1)} %get-tuple-element.94) | copy-start | bytes 18436
  15.5 11.5 %copy-start.74 = (f32[1536]{0:T(1024)}, f32[1536]{0:T(1024)S(1)}, u32[]{:S(2)}) copy-start(f32[1536]{0:T(1024)S(1)} %get-tuple-element.95) | copy-start | bytes 18436
  15.5 11.5 %copy-start.76 = (f32[1536]{0:T(1024)}, f32[1536]{0:T(1024)S(1)}, u32[]{:S(2)}) copy-start(f32[1536]{0:T(1024)S(1)} %get-tuple-element.96) | copy-start | bytes 18436
  15.5 11.5 %copy-start.78 = (f32[1536]{0:T(1024)}, f32[1536]{0:T(1024)S(1)}, u32[]{:S(2)}) copy-start(f32[1536]{0:T(1024)S(1)} %get-tuple-element.97) | copy-start | bytes 18436
  15.6 11.5 %copy-start.80 = (f32[1536]{0:T(1024)}, f32[1536]{0:T(1024)S(1)}, u32[]{:S(2)}) copy-start(f32[1536]{0:T(1024)S(1)} %get-tuple-element.98) | copy-start | bytes 18436
  15.6 11.5 %copy-start.82 = (f32[1536]{0:T(1024)}, f32[1536]{0:T(1024)S(1)}, u32[]{:S(2)}) copy-start(f32[1536]{0:T(1024)S(1)} %get-tuple-element.99) | copy-start | bytes 18436
  42.1 82.8 %reduce-scatter.7.cloned.1.call-start = ((), (), s32[]{:S(2)}) async-start(), calls=%async_computation.3 | async-start | bytes 5898240
  53.6 106.1 %reduce-scatter.5.cloned.1.call-start = ((), (), s32[]{:S(2)}) async-start(), calls=%async_computation.2 | async-start | bytes 5898240 | tf_op jit(solution)/shard_map/reduce_scatter | solution.py:90
  58.5 32.9 %copy-start.84 = (f32[128]{0:T(128)S(1)}, f32[128]{0:T(128)}, u32[]{:S(2)}) copy-start(f32[128]{0:T(128)} %div.15) | copy-start | bytes 1540
  58.5 32.9 %copy-start.85 = (f32[128]{0:T(128)S(1)}, f32[128]{0:T(128)}, u32[]{:S(2)}) copy-start(f32[128]{0:T(128)} %rsqrt.12) | copy-start | bytes 1540
  99.5 15.2 %copy-start.7 = (bf16[128,1536]{1,0:T(8,128)(2,1)S(1)}, bf16[128,1536]{1,0:T(8,128)(2,1)}, u32[]{:S(2)}) copy-start(bf16[128,1536]{1,0:T(8,128)(2,1)} %get-tuple-element.114) | copy-start | bytes 1179652
  111.0 4.5 %collective-permute-start.2 = (bf16[3,32,1536]{2,1,0:T(8,128)(2,1)S(1)}, bf16[3,32,1536]{2,1,0:T(8,128)(2,1)S(1)}, u32[]{:S(2)}, u32[]{:S(2)}) collective-permute-start(bf16[3,32,1536]{2,1,0:T(8,128)(2,1)S(1)} %bitcast.93), channel_id=1, source_target_pairs={{0,1},{1,2},{2,3},{4,5},{5,6},{6,7},{8,9},{9,10},{10,11},{12,13},{... | collective-permute-start | bytes 884744 | tf_op jit(solution)/shard_map/ppermute | solution.py:19
  113.3 3.5 %collective-permute-start.3 = (bf16[3,32,1536]{2,1,0:T(8,128)(2,1)S(1)}, bf16[3,32,1536]{2,1,0:T(8,128)(2,1)S(1)}, u32[]{:S(2)}, u32[]{:S(2)}) collective-permute-start(bf16[3,32,1536]{2,1,0:T(8,128)(2,1)S(1)} %bitcast.92), channel_id=1, source_target_pairs={{1,0},{2,1},{3,2},{5,4},{6,5},{7,6},{9,8},{10,9},{11,10},{13,12},{... | collective-permute-start | bytes 884744 | tf_op jit(solution)/shard_map/ppermute | solution.py:22
  (73 other events, 444.8 us)
Sparse Core Ops, SparseCore 0:
  42.2 49.0 all-reduce.4
Sparse Core Ops, SparseCore 1:
  53.7 53.9 reduce-scatter.6
  110.2 49.4 reduce-scatter.4
